TPU v7x, 512 devices: a whole 4x4x16 slice. The times are simulated.
512 devices in a mesh: gx: 16 (over z), gy: 8 (over x, core), gz: 4 (over y).
Axes of the slice: x: 4, y: 4, z: 16, core: 2. Of those that a mesh axis runs over, the one named last changes fastest.
Arguments:
- populations: float32 [19, 64, 64, 512], P(None, 'gx', 'gy', 'gz'), may hold values from 0.02 to 0.09
- solid_cells: int32 [64, 64, 512], P('gx', 'gy', 'gz'), may hold values 0 or 1
- slot_cells: int32 [16, 8, 4, 64, 8, 128], P('gx', 'gy', 'gz'), may hold values from 0 to 4095
- slot_weights: float32 [16, 8, 4, 64, 8, 128], P('gx', 'gy', 'gz'), may hold values from 0 to 0.0625
- slot_owner: int32 [16, 8, 4, 64, 1], P('gx', 'gy', 'gz'), may hold values from 0 to 127; in each aligned block of 64 rows (0 to 63, 64 to 127, ..., all dimensions but the last counted through in order) at most 2 rows name the same one
- slot_block: int32 [16, 8, 4, 64], P('gx', 'gy', 'gz'), may hold values from 0 to 31
- train_of_block: int32 [16, 8, 4, 32], P('gx', 'gy', 'gz'), may hold values from 0 to 3
- marker_area: float32 [16, 8, 4, 32, 128], P('gx', 'gy', 'gz'), may hold values from 0.5 to 2
- train_velocity: float32 [4, 3], replicated, may hold values from -0.1 to 0.1
Outputs:
- populations_next: float32 [19, 64, 64, 512], P(None, 'gx', 'gy', 'gz')
- marker_force: float32 [16, 8, 4, 32, 3, 128], P('gx', 'gy', 'gz')
Inputs may be any that keep to these rules, and one draw needn't show every extreme that they name: `slot_owner`: among the 64 slots of one device no owner is named more than 2 times, a bound that some block reaches.
All inputs are finite; a program needn't handle non-finite values. No bound on the sum of `solid_cells` on one device may be relied on, other than what follows from the above.
Results may differ from a plain program's by a relative error of at most 0.000065.
Values sent between devices are 32-bit elements; how exact they have to be, the bound alone decides.
A program may use at most 128 MiB of HBM per device.

v0:
```python
import jax
import jax.numpy as jnp
import numpy as np
from jax import lax
from jax.sharding import PartitionSpec as P

velocity_table = np.array(
    [
        [0, 0, 0],
        [1, 0, 0],
        [-1, 0, 0],
        [0, 1, 0],
        [0, -1, 0],
        [0, 0, 1],
        [0, 0, -1],
        [1, 1, 0],
        [-1, -1, 0],
        [1, -1, 0],
        [-1, 1, 0],
        [1, 0, 1],
        [-1, 0, -1],
        [1, 0, -1],
        [-1, 0, 1],
        [0, 1, 1],
        [0, -1, -1],
        [0, 1, -1],
        [0, -1, 1],
    ]
)
weight_table = [1.0 / 3.0] + [1.0 / 18.0] * 6 + [1.0 / 36.0] * 12
opposite_table = [0, 2, 1, 4, 3, 6, 5, 8, 7, 10, 9, 12, 11, 14, 13, 16, 15, 18, 17]
stress_pairs = [(0, 0), (1, 1), (2, 2), (0, 1), (0, 2), (1, 2)]
tau_base = 0.55
smag_term = 18.0 * 1.4142135623730951 * 0.17 * 0.17
regular_eps = 0.0001
stiffness = 2.0
far_velocity = (0.02, 0.06, 0.0)


def with_halo(cells, sides, width):
    for axis, dim in sides:
        count = lax.axis_size(axis)
        head = lax.slice_in_dim(cells, 0, width, axis=dim)
        tail = lax.slice_in_dim(cells, cells.shape[dim] - width, cells.shape[dim], axis=dim)
        cells = jnp.concatenate(
            [
                lax.ppermute(tail, axis, [(i, (i + 1) % count) for i in range(count)]),
                cells,
                lax.ppermute(head, axis, [((i + 1) % count, i) for i in range(count)]),
            ],
            axis=dim,
        )
    return cells


def project(direction, vector):
    projection = 0.0 * vector[0]
    for component in range(3):
        lattice_step = int(velocity_table[direction][component])
        if lattice_step != 0:
            projection = projection + lattice_step * vector[component]
    return projection


def moments(populations):
    density = populations[0]
    momentum = [jnp.zeros_like(density) for component in range(3)]
    for direction in range(1, 19):
        density = density + populations[direction]
        for component in range(3):
            lattice_step = int(velocity_table[direction][component])
            if lattice_step == 1:
                momentum[component] = momentum[component] + populations[direction]
            elif lattice_step == -1:
                momentum[component] = momentum[component] - populations[direction]
    return (density, momentum)


def equilibrium(density, velocity):
    speed_sq = velocity[0] * velocity[0] + velocity[1] * velocity[1] + velocity[2] * velocity[2]
    result = []
    for direction in range(19):
        projected = project(direction, velocity)
        result.append(
            weight_table[direction]
            * density
            * (1.0 + 3.0 * projected + 4.5 * projected * projected - 1.5 * speed_sq)
        )
    return result


def collide(populations, cell_force, solid_cells):
    density, momentum = moments(populations)
    velocity = [
        (momentum[component] + 0.5 * cell_force[component]) / density for component in range(3)
    ]
    balance = equilibrium(density, velocity)
    stress = [jnp.zeros_like(density) for pair_pos in range(6)]
    for direction in range(19):
        non_eq = populations[direction] - balance[direction]
        for pair_pos in range(6):
            row_axis, col_axis = stress_pairs[pair_pos]
            factor = int(velocity_table[direction][row_axis] * velocity_table[direction][col_axis])
            if factor != 0:
                stress[pair_pos] = stress[pair_pos] + factor * non_eq
    shear_sq = stress[0] * stress[0] + stress[1] * stress[1] + stress[2] * stress[2]
    shear_sq = shear_sq + 2.0 * (
        stress[3] * stress[3] + stress[4] * stress[4] + stress[5] * stress[5]
    )
    magnitude = jnp.sqrt(shear_sq + regular_eps)
    relax_time = 0.5 * (tau_base + jnp.sqrt(tau_base * tau_base + smag_term * magnitude / density))
    guo_factor = 1.0 - 0.5 / relax_time
    speed_force = (
        velocity[0] * cell_force[0] + velocity[1] * cell_force[1] + velocity[2] * cell_force[2]
    )
    result = []
    for direction in range(19):
        along_force = project(direction, cell_force)
        along_speed = project(direction, velocity)
        source = (
            guo_factor
            * weight_table[direction]
            * (3.0 * (along_force - speed_force) + 9.0 * along_speed * along_force)
        )
        relaxed = (
            populations[direction]
            - (populations[direction] - balance[direction]) / relax_time
            + source
        )
        result.append(jnp.where(solid_cells == 1, populations[opposite_table[direction]], relaxed))
    return jnp.stack(result)


def settle(received, labels, owned, train_of_block, marker_area, train_velocity, mark):
    rows_in = received.reshape(-1, 3 * mark)
    label_rows = labels.reshape(-1)
    owner_match = (label_rows[None, :] == jnp.arange(owned, dtype=jnp.int32)[:, None]).astype(
        jnp.float32
    )
    marker_velocity = jnp.dot(owner_match, rows_in, precision=lax.Precision.HIGHEST).reshape(
        owned, 3, mark
    )
    trains = train_velocity.shape[0]
    train_rows = train_of_block.reshape(owned)
    train_match = (train_rows[:, None] == jnp.arange(trains, dtype=jnp.int32)[None, :]).astype(
        jnp.float32
    )
    target = jnp.dot(train_match, train_velocity, precision=lax.Precision.HIGHEST)
    areas = marker_area.reshape(owned, mark)
    marker_force = stiffness * areas[:, None, :] * (target[:, :, None] - marker_velocity)
    back_rows = jnp.dot(
        owner_match.T, marker_force.reshape(owned, 3 * mark), precision=lax.Precision.HIGHEST
    )
    return (marker_force, back_rows)


def per_device(
    populations,
    solid_cells,
    slot_cells,
    slot_weights,
    slot_owner,
    slot_block,
    train_of_block,
    marker_area,
    train_velocity,
):
    size_x, size_y, size_z = (populations.shape[1], populations.shape[2], populations.shape[3])
    cell_count = size_x * size_y * size_z
    slots, kernel, mark = (slot_cells.shape[3], slot_cells.shape[4], slot_cells.shape[5])
    owned = train_of_block.shape[3]
    peers_x = lax.axis_size("gx")
    peers_y = lax.axis_size("gy")
    peers = peers_x * peers_y
    capacity = max(2, 2 * slots // peers)
    density, momentum = moments(populations)
    rest_velocity = jnp.stack([momentum[component] / density for component in range(3)]).reshape(
        3, cell_count
    )
    cells = slot_cells.reshape(slots, kernel, mark)
    weights = slot_weights.reshape(slots, kernel, mark)
    partial_value = jnp.sum(rest_velocity[:, cells] * weights[None], axis=2)
    slot_rows = partial_value.transpose(1, 0, 2).reshape(slots, 3 * mark)
    slot_dest = slot_owner.reshape(slots)
    blocks = slot_block.reshape(slots)
    order = jnp.arange(slots, dtype=jnp.int32)
    earlier = (slot_dest[None, :] == slot_dest[:, None]) & (order[None, :] < order[:, None])
    slot_rank = jnp.sum(earlier.astype(jnp.int32), axis=1)
    target_row = slot_dest * capacity + slot_rank
    buffer_rows = jnp.arange(peers * capacity, dtype=jnp.int32)
    matches = buffer_rows[:, None] == target_row[None, :]
    placement = matches.astype(jnp.float32)
    outgoing = jnp.dot(placement, slot_rows, precision=lax.Precision.HIGHEST)
    labels = jnp.sum(jnp.where(matches, blocks[None, :] + 1, 0), axis=1) - 1
    received, got_labels = (
        lax.all_to_all(
            outgoing.reshape(peers, capacity, 3 * mark),
            ("gx", "gy"),
            split_axis=0,
            concat_axis=0,
            tiled=True,
        ),
        lax.all_to_all(
            labels.reshape(peers, capacity), ("gx", "gy"), split_axis=0, concat_axis=0, tiled=True
        ),
    )
    marker_force, back_rows = settle(
        received, got_labels, owned, train_of_block, marker_area, train_velocity, mark
    )
    returned = lax.all_to_all(
        back_rows.reshape(peers, capacity, 3 * mark),
        ("gx", "gy"),
        split_axis=0,
        concat_axis=0,
        tiled=True,
    )
    slot_force = jnp.dot(
        placement.T, returned.reshape(peers * capacity, 3 * mark), precision=lax.Precision.HIGHEST
    )
    slot_force = slot_force.reshape(slots, 3, mark).transpose(1, 0, 2)
    contrib = weights[None] * slot_force[:, :, None, :]
    cell_force = (
        jnp.zeros((3, cell_count), jnp.float32).at[:, cells.reshape(-1)].add(contrib.reshape(3, -1))
    )
    cell_force = cell_force.reshape(3, size_x, size_y, size_z)
    relaxed = collide(populations, cell_force, solid_cells)
    padded = with_halo(relaxed, (("gx", 1), ("gy", 2), ("gz", 3)), 1)
    parts = []
    for direction in range(19):
        shift_x = 1 - int(velocity_table[direction][0])
        shift_y = 1 - int(velocity_table[direction][1])
        shift_z = 1 - int(velocity_table[direction][2])
        parts.append(
            padded[
                direction,
                shift_x : shift_x + size_x,
                shift_y : shift_y + size_y,
                shift_z : shift_z + size_z,
            ]
        )
    read = jnp.stack(parts)
    total_y = size_y * lax.axis_size("gy")
    total_z = size_z * lax.axis_size("gz")
    global_y = lax.axis_index("gy") * size_y + jnp.arange(size_y, dtype=jnp.int32)
    global_z = lax.axis_index("gz") * size_z + jnp.arange(size_z, dtype=jnp.int32)
    on_side = ((global_y == 0) | (global_y == total_y - 1))[:, None] | (
        (global_z == 0) | (global_z == total_z - 1)
    )[None, :]
    far_field = jnp.array(equilibrium(1.0, list(far_velocity)), dtype=jnp.float32)
    populations_next = jnp.where(on_side[None, None], far_field[:, None, None, None], read)
    return (populations_next, marker_force.reshape(1, 1, 1, owned, 3, mark))


def solution(mesh):
    placed = (
        P(None, "gx", "gy", "gz"),
        P("gx", "gy", "gz"),
        P("gx", "gy", "gz", None, None, None),
        P("gx", "gy", "gz", None, None, None),
        P("gx", "gy", "gz", None, None),
        P("gx", "gy", "gz", None),
        P("gx", "gy", "gz", None),
        P("gx", "gy", "gz", None, None),
        P(),
    )
    return jax.shard_map(
        per_device,
        mesh=mesh,
        in_specs=placed,
        out_specs=(P(None, "gx", "gy", "gz"), P("gx", "gy", "gz", None, None, None)),
        check_vma=False,
    )
```

profile of v0, /device:TPU:1, one launch (start us, length us, event | category | flops | bytes accessed | tf_op | source)
XLA Modules:
  0.0 717.3 jit_solution(3256920983020927169)
XLA Ops:
  3.8 20.4 %all-to-all-start = ((s32[128,1,2]{2,1,0:T(1,128)}), s32[128,1,2]{2,1,0:T(1,128)S(1)}, u32[]{:S(2)}, u32[]{:S(2)}) async-start(s32[128,1,2]{2,1,0:T(1,128)} %bitcast.25), calls=%async_computation | async-start | bytes 131072 | tf_op jit(solution)/shard_map/all_to_all | solution.py:203
  27.6 1.1 fusion.5
  28.7 216.0 %gather_fusion = f32[65536,3]{1,0:T(8,128)} fusion(f32[3,4096]{0,1:T(8,128)S(1)} %copy.39, s32[65536]{0:T(1024)S(1)} %fusion.5), kind=kCustom, calls=%fused_computation | custom fusion | bytes 1835008 | tf_op jit(solution)/shard_map/gather | solution.py:182
  244.6 14.0 %multiply_reduce_fusion = f32[64,128,3]{2,1,0:T(8,128)} fusion(f32[64,8,128,3]{3,2,1,0:T(8,128)} %bitcast.680, f32[64,8,128]{2,1,0:T(8,128)S(1)} %bitcast.686), kind=kLoop, calls=%fused_computation.5 | loop fusion | flops 368640 | bytes 1146880 | tf_op jit(solution)/shard_map/reduce_sum | solution.py:182
  258.6 2.9 copy.40
  263.1 16.1 %all-to-all-start.1 = ((f32[128,2,384]{2,1,0:T(2,128)}), f32[128,2,384]{2,1,0:T(2,128)S(1)}, u32[]{:S(2)}, u32[]{:S(2)}) async-start(f32[128,2,384]{2,1,0:T(2,128)} %copy.41), calls=%async_computation.1 | async-start | bytes 786432 | tf_op jit(solution)/shard_map/all_to_all | solution.py:196
  280.9 23.7 %all-to-all-done.1 = f32[128,2,384]{2,1,0:T(2,128)S(1)} async-done(((f32[128,2,384]{2,1,0:T(2,128)}), f32[128,2,384]{2,1,0:T(2,128)S(1)}, u32[]{:S(2)}, u32[]{:S(2)}) %all-to-all-start.1) | async-done | bytes 393248 | tf_op jit(solution)/shard_map/all_to_all | solution.py:196
  306.9 8.9 %all-to-all-start.2 = ((f32[128,2,384]{2,1,0:T(2,128)}), f32[128,2,384]{2,1,0:T(2,128)S(1)}, u32[]{:S(2)}, u32[]{:S(2)}) async-start(f32[128,2,384]{2,1,0:T(2,128)} %copy.44), calls=%async_computation.2 | async-start | bytes 786432 | tf_op jit(solution)/shard_map/all_to_all | solution.py:210
  316.2 25.1 %all-to-all-done.2 = f32[128,2,384]{2,1,0:T(2,128)S(1)} async-done(((f32[128,2,384]{2,1,0:T(2,128)}), f32[128,2,384]{2,1,0:T(2,128)S(1)}, u32[]{:S(2)}, u32[]{:S(2)}) %all-to-all-start.2) | async-done | bytes 393248 | tf_op jit(solution)/shard_map/all_to_all | solution.py:210
  342.1 2.7 copy.46
  344.8 12.8 %bitcast_multiply_fusion = f32[3,65536]{0,1:T(8,128)} fusion(f32[3,64,128]{0,2,1:T(8,128)} %copy.46, f32[65536]{0:T(1024)S(1)} %bitcast.687), kind=kLoop, calls=%fused_computation.4 | loop fusion | flops 196608 | bytes 1146880 | tf_op jit(solution)/shard_map/mul | solution.py:221
  357.6 316.3 %scatter_custom_fusion = f32[3,4096]{0,1:T(8,128)S(1)} fusion(s32[65536]{0:T(1024)S(1)} %bitcast.690, f32[3,65536]{0,1:T(8,128)} %bitcast_multiply_fusion, f32[]{:T(128)} %constant.10.clone.1), kind=kCustom, calls=%fused_computation.2 | custom fusion | flops 196608 | bytes 835588 | tf_op jit(solution)/shard_map/scatter-add | solution.py:223
  673.9 2.8 slice_reduce_fusion.1
  677.7 6.0 collective-permute-start
  683.7 1.9 collective-permute-start.1
  685.7 3.6 collective-permute-done.1
  689.4 1.3 collective-permute-start.2
  690.7 1.2 collective-permute-done.2
  692.0 2.6 collective-permute-done.3
  695.7 3.2 collective-permute-start.4
  699.5 3.4 collective-permute-start.5
  704.1 1.1 copy.48
  705.1 1.1 copy.50
  715.5 1.8 broadcast_select_fusion
  (107 shorter events, 26.3 us)
Async XLA Ops:
  0.6 278.6 %copy-start = (f32[4,3]{1,0:T(4,128)S(1)}, f32[4,3]{1,0:T(4,128)}, u32[]{:S(2)}) copy-start(f32[4,3]{1,0:T(4,128)} %param.18) | copy-start | bytes 148
  3.8 259.3 %all-to-all-start = ((s32[128,1,2]{2,1,0:T(1,128)}), s32[128,1,2]{2,1,0:T(1,128)S(1)}, u32[]{:S(2)}, u32[]{:S(2)}) async-start(s32[128,1,2]{2,1,0:T(1,128)} %bitcast.25), calls=%async_computation | async-start | bytes 131072 | tf_op jit(solution)/shard_map/all_to_all | solution.py:203
  27.6 217.0 %copy-start.4 = (f32[1,1,1,64,8,128]{5,4,3,2,1,0:T(8,128)S(1)}, f32[1,1,1,64,8,128]{5,4,3,2,1,0:T(8,128)}, u32[]{:S(2)}) copy-start(f32[1,1,1,64,8,128]{5,4,3,2,1,0:T(8,128)} %param.13) | copy-start | bytes 786436
  258.6 20.6 %copy-start.10 = (s32[1,1,1,32]{3,2,1,0:T(1,128)S(1)}, s32[1,1,1,32]{3,2,1,0:T(1,128)}, u32[]{:S(2)}) copy-start(s32[1,1,1,32]{3,2,1,0:T(1,128)} %param.16) | copy-start | bytes 388
  258.6 20.8 %copy-start.8 = (f32[1,1,1,32,128]{4,3,2,1,0:T(8,128)S(1)}, f32[1,1,1,32,128]{4,3,2,1,0:T(8,128)}, u32[]{:S(2)}) copy-start(f32[1,1,1,32,128]{4,3,2,1,0:T(8,128)} %param.17) | copy-start | bytes 49156
  261.5 54.3 %copy-start.5 = (s32[1,1,1,64,8,128]{5,4,3,2,1,0:T(8,128)S(1)}, s32[1,1,1,64,8,128]{5,4,3,2,1,0:T(8,128)}, u32[]{:S(2)}) copy-start(s32[1,1,1,64,8,128]{5,4,3,2,1,0:T(8,128)} %param.12) | copy-start | bytes 786436
  263.1 41.6 %all-to-all-start.1 = ((f32[128,2,384]{2,1,0:T(2,128)}), f32[128,2,384]{2,1,0:T(2,128)S(1)}, u32[]{:S(2)}, u32[]{:S(2)}) async-start(f32[128,2,384]{2,1,0:T(2,128)} %copy.41), calls=%async_computation.1 | async-start | bytes 786432 | tf_op jit(solution)/shard_map/all_to_all | solution.py:196
  305.4 39.4 %copy-start.6 = (f32[32,3,128]{2,0,1:T(8,128)}, f32[32,3,128]{2,0,1:T(8,128)S(1)}, u32[]{:S(2)}) copy-start(f32[32,3,128]{2,0,1:T(8,128)S(1)} %fusion.2) | copy-start | bytes 147460
  306.9 34.4 %all-to-all-start.2 = ((f32[128,2,384]{2,1,0:T(2,128)}), f32[128,2,384]{2,1,0:T(2,128)S(1)}, u32[]{:S(2)}, u32[]{:S(2)}) async-start(f32[128,2,384]{2,1,0:T(2,128)} %copy.44), calls=%async_computation.2 | async-start | bytes 786432 | tf_op jit(solution)/shard_map/all_to_all | solution.py:210
  673.9 2.8 copy-start.2
  673.9 2.8 copy-start.7
  677.7 8.0 %collective-permute-start = (f32[19,1,8,128]{3,2,1,0:T(8,128)S(1)}, f32[19,1,8,128]{3,2,1,0:T(8,128)S(1)}, u32[]{:S(2)}, u32[]{:S(2)}) collective-permute-start(f32[19,1,8,128]{3,2,1,0:T(8,128)S(1)} %get-tuple-element.20), channel_id=1, source_target_pairs={{0,32},{32,64},{64,96},{96,128},{128,160},{160,192},{192,224},{224... | collective-permute-start | bytes 233480 | tf_op jit(solution)/shard_map/ppermute | solution.py:47
  683.7 5.6 collective-permute-start.1
  689.4 2.6 collective-permute-start.2
  690.7 3.9 collective-permute-start.3
  690.7 1.3 copy-start.3
  695.7 8.3 %collective-permute-start.4 = (f32[19,6,10,1]{0,3,2,1:T(1,128)S(1)}, f32[19,6,10,1]{0,3,2,1:T(1,128)S(1)}, u32[]{:S(2)}, u32[]{:S(2)}) collective-permute-start(f32[19,6,10,1]{0,3,2,1:T(1,128)S(1)} %copy.47), channel_id=1, source_target_pairs={{0,1},{1,2},{2,3},{3,0},{4,5},{5,6},{6,7},{7,4},{8,9},{9,10},{10,1... | collective-permute-start | bytes 13688 | tf_op jit(solution)/shard_map/ppermute | solution.py:47
  699.5 5.6 collective-permute-start.5
  711.4 5.9 copy-start.1
  712.1 3.4 copy-start.9
where the time goes:
time: 718 us; the launch traced here: 717 us
  other arithmetic  364 us (51%)
  local copies, waits for them, and re-layouts  233 us (32%)
  starting transfers between devices  61.2 us (9%)
  waiting for transfers between devices  56.3 us (8%)
    scatter-add x1, other arithmetic, per_device(): jnp.zeros((3, cell_count), jnp.float32).at[:, cells.reshape(-1)]  316 us
    gather x1, local copies, waits for them, and re-layouts, per_device(): partial_value = jnp.sum(rest_velocity[:, cells] * weights[None], axis=2)  216 us
    all_to_all x1, waiting for transfers between devices, per_device(): lax.all_to_all(back_rows.reshape(peers, capacity, 3 * mark), ('gx', 'gy')...  25.1 us
    all_to_all x1, waiting for transfers between devices, per_device(): lax.all_to_all(outgoing.reshape(peers, capacity, 3 * mark), ('gx', 'gy'),...  23.7 us
    all_to_all x1, starting transfers between devices, per_device(): lax.all_to_all(labels.reshape(peers, capacity), ('gx', 'gy'), split_axis=...  20.4 us
    all_to_all x1, starting transfers between devices, per_device(): lax.all_to_all(outgoing.reshape(peers, capacity, 3 * mark), ('gx', 'gy'),...  16.1 us
  transfers between devices with their start and end apart: 9, of which 5 were waited for; matrix products, arithmetic and copies ran while one was open for 34% of the time, Pallas kernels for 0%

commit v1 on v0

v1 whole, which is shorter than its diff:
```python
import functools

import jax
import jax.numpy as jnp
import numpy as np
from jax import lax
from jax.experimental import pallas as pl
from jax.experimental.pallas import tpu as pltpu
from jax.sharding import PartitionSpec as P

velocity_table = np.array(
    [
        [0, 0, 0],
        [1, 0, 0],
        [-1, 0, 0],
        [0, 1, 0],
        [0, -1, 0],
        [0, 0, 1],
        [0, 0, -1],
        [1, 1, 0],
        [-1, -1, 0],
        [1, -1, 0],
        [-1, 1, 0],
        [1, 0, 1],
        [-1, 0, -1],
        [1, 0, -1],
        [-1, 0, 1],
        [0, 1, 1],
        [0, -1, -1],
        [0, 1, -1],
        [0, -1, 1],
    ]
)
weight_table = [1.0 / 3.0] + [1.0 / 18.0] * 6 + [1.0 / 36.0] * 12
opposite_table = [0, 2, 1, 4, 3, 6, 5, 8, 7, 10, 9, 12, 11, 14, 13, 16, 15, 18, 17]
stress_pairs = [(0, 0), (1, 1), (2, 2), (0, 1), (0, 2), (1, 2)]
tau_base = 0.55
smag_term = 18.0 * 1.4142135623730951 * 0.17 * 0.17
regular_eps = 0.0001
stiffness = 2.0
far_velocity = (0.02, 0.06, 0.0)
MESH = pl.DeviceIdType.MESH
f32 = jnp.float32
bf16 = jnp.bfloat16
i32 = jnp.int32

facing = [
    {sign: [q for q in range(19) if velocity_table[q][axis] == sign] for sign in (1, -1)}
    for axis in range(3)
]
Z_SIDES = ((0, 0), (1, 0), (-1, 0), (0, 1), (0, -1))
Y_SIDES = (0, 1, -1)


def project(direction, vector):
    projection = None
    for component in range(3):
        lattice_step = int(velocity_table[direction][component])
        if lattice_step != 0:
            term = vector[component] if lattice_step == 1 else -vector[component]
            projection = term if projection is None else projection + term
    return projection


def moments(populations):
    density = populations[0]
    momentum = [None, None, None]
    for direction in range(1, 19):
        density = density + populations[direction]
        for component in range(3):
            lattice_step = int(velocity_table[direction][component])
            if lattice_step != 0:
                term = populations[direction] if lattice_step == 1 else -populations[direction]
                momentum[component] = (
                    term if momentum[component] is None else momentum[component] + term
                )
    return (density, momentum)


def equilibrium(density, velocity):
    speed_sq = velocity[0] * velocity[0] + velocity[1] * velocity[1] + velocity[2] * velocity[2]
    base = 1.0 - 1.5 * speed_sq
    result = []
    for direction in range(19):
        projected = project(direction, velocity)
        inner = base if projected is None else base + projected * (3.0 + 4.5 * projected)
        result.append(weight_table[direction] * density * inner)
    return result


def far_field():
    speed_sq = sum(v * v for v in far_velocity)
    values = []
    for direction in range(19):
        projected = sum(int(velocity_table[direction][i]) * far_velocity[i] for i in range(3))
        values.append(
            weight_table[direction]
            * (1.0 + 3.0 * projected + 4.5 * projected * projected - 1.5 * speed_sq)
        )
    return values


def collide(populations, cell_force, solid):
    density, momentum = moments(populations)
    inverse = 1.0 / density
    velocity = [
        (momentum[component] + 0.5 * cell_force[component]) * inverse for component in range(3)
    ]
    balance = equilibrium(density, velocity)
    stress = [None] * 6
    departure = []
    for direction in range(19):
        non_eq = populations[direction] - balance[direction]
        departure.append(non_eq)
        for pair_pos in range(6):
            row_axis, col_axis = stress_pairs[pair_pos]
            factor = int(velocity_table[direction][row_axis] * velocity_table[direction][col_axis])
            if factor != 0:
                term = non_eq if factor == 1 else -non_eq
                stress[pair_pos] = term if stress[pair_pos] is None else stress[pair_pos] + term
    shear_sq = stress[0] * stress[0] + stress[1] * stress[1] + stress[2] * stress[2]
    shear_sq = shear_sq + 2.0 * (
        stress[3] * stress[3] + stress[4] * stress[4] + stress[5] * stress[5]
    )
    magnitude = jnp.sqrt(shear_sq + regular_eps)
    relax_time = 0.5 * (tau_base + jnp.sqrt(tau_base * tau_base + smag_term * magnitude * inverse))
    rate = 1.0 / relax_time
    guo_factor = 1.0 - 0.5 * rate
    speed_force = (
        velocity[0] * cell_force[0] + velocity[1] * cell_force[1] + velocity[2] * cell_force[2]
    )
    base = -3.0 * speed_force
    result = []
    for direction in range(19):
        along_force = project(direction, cell_force)
        along_speed = project(direction, velocity)
        inner = base if along_force is None else base + along_force * (3.0 + 9.0 * along_speed)
        relaxed = (
            populations[direction]
            - departure[direction] * rate
            + (guo_factor * weight_table[direction]) * inner
        )
        result.append(jnp.where(solid, populations[opposite_table[direction]], relaxed))
    return result


def pick_rows(one_hot, values):
    high = values.astype(bf16)
    rest = values - high.astype(f32)
    middle = rest.astype(bf16)
    low = (rest - middle.astype(f32)).astype(bf16)
    total = jnp.dot(one_hot, low, preferred_element_type=f32)
    total = total + jnp.dot(one_hot, middle, preferred_element_type=f32)
    return total + jnp.dot(one_hot, high, preferred_element_type=f32)


def iota(shape, dim):
    return lax.broadcasted_iota(i32, shape, dim)


def hot(condition):
    return jnp.where(condition, 1.0, 0.0).astype(bf16)


def to_column(row):
    n = row.shape[1]
    square = jnp.broadcast_to(row, (n, n))
    return jnp.sum(jnp.where(iota((n, n), 0) == iota((n, n), 1), square, 0.0), axis=1, keepdims=True)


def kernel(
    px,
    py,
    pz,
    pop,
    solid,
    cells,
    weights,
    owner,
    block,
    train,
    area,
    speed,
    out,
    force_out,
    table,
    rows,
    place,
    place_t,
    combine,
    combine_t,
    lab_send,
    lab_recv,
    z_send,
    z_recv,
    d_send,
    d_recv,
    f_all,
    r_send,
    r_recv,
    lane_hot,
    cell_force,
    relaxed,
    x_send,
    x_recv,
    y_send,
    y_recv,
    t_send,
    t_recv,
    send_sem,
    recv_sem,
    halo_send,
    halo_recv,
):
    slots, kern, mark = cells.shape
    size_x, size_y, size_z = pop.shape[1:]
    own = area.shape[0]
    cap = 2
    per_plane = py * cap
    total_rows = px * per_plane
    row_count = size_x * size_y
    gx, gy, gz = lax.axis_index("gx"), lax.axis_index("gy"), lax.axis_index("gz")

    def at(dx, dy, dz):
        return (
            lax.rem(gx + px + dx, px),
            lax.rem(gy + py + dy, py),
            lax.rem(gz + pz + dz, pz),
        )

    halo_far = (
        [(0, 0, s) for s in (1, -1)]
        + [(a, b, 0) for a in (1, -1) for b in (1, -1)]
        + [(a, 0, b) for a in (1, -1) for b in (1, -1)]
        + [(0, a, b) for a in (1, -1) for b in (1, -1)]
    )
    barrier = pltpu.get_barrier_semaphore()

    def greet_x(k, _):
        pl.semaphore_signal(barrier, inc=1, device_id=at(k, 0, 0), device_id_type=MESH)
        return 0

    def greet_y(k, _):
        pl.semaphore_signal(barrier, inc=1, device_id=at(0, k, 0), device_id_type=MESH)
        return 0

    lax.fori_loop(1, px, greet_x, 0)
    lax.fori_loop(1, py, greet_y, 0)
    for place_of in halo_far:
        pl.semaphore_signal(barrier, inc=1, device_id=at(*place_of), device_id_type=MESH)

    owner_row = owner[...].astype(f32)
    owner_col = to_column(owner_row)
    same = owner_col == owner_row
    first, second = iota((slots, slots), 0), iota((slots, slots), 1)
    rank_row = jnp.sum(jnp.where(same & (first < second), 1.0, 0.0), axis=0, keepdims=True)
    rank_col = jnp.sum(jnp.where(same & (second < first), 1.0, 0.0), axis=1, keepdims=True)
    target_row = (owner_row * cap + rank_row).astype(i32)
    target_col = (owner_col * cap + rank_col).astype(i32)
    place[...] = hot(iota((total_rows, slots), 0) == target_row)
    place_t[...] = hot(iota((slots, total_rows), 1) == target_col)
    label_col = to_column(block[...].astype(f32)) + 1.0
    half = mark // per_plane
    plane_hot = hot(iota((px, slots), 0) == target_row // per_plane)
    spot = lax.rem(target_col, per_plane) + per_plane * lax.rem(gx, half)
    label_hot = jnp.where(iota((slots, mark), 1) == spot, label_col, 0.0).astype(bf16)
    labels = jnp.dot(plane_hot, label_hot, preferred_element_type=f32)
    lab_send[...] = jnp.broadcast_to(labels[:, None, :], lab_send.shape)
    lab_recv[gx] = lab_send[gx]

    density, momentum = moments([pop[q] for q in range(19)])
    for c in range(3):
        table[c] = (momentum[c] / density).reshape(row_count, size_z)

    pl.semaphore_wait(barrier, px - 1 + py - 1 + len(halo_far))

    def send_x(source, target, stage):
        def step(i, _):
            k = px // 2 + ((i + 1) // 2) * (1 - 2 * lax.rem(i, 2))
            peer = at(k, 0, 0)
            pltpu.make_async_remote_copy(
                src_ref=source.at[peer[0]],
                dst_ref=target.at[gx],
                send_sem=send_sem.at[stage],
                recv_sem=recv_sem.at[stage],
                device_id=peer,
                device_id_type=MESH,
            ).start()
            return 0

        lax.fori_loop(0, px - 1, step, 0)

    def send_y(source, own_place, target, stage):
        def step(k, _):
            peer = at(0, k, 0)
            pltpu.make_async_remote_copy(
                src_ref=source.at[gy if own_place else peer[1]],
                dst_ref=target.at[gy],
                send_sem=send_sem.at[stage],
                recv_sem=recv_sem.at[stage],
                device_id=peer,
                device_id_type=MESH,
            ).start()
            return 0

        lax.fori_loop(1, py, step, 0)

    def wait_for(buffer, count, semaphore):
        part = buffer.at[pl.ds(0, count)]
        pltpu.make_async_copy(part, part, semaphore).wait()

    LAB, ZS, DS, FS, RS = 0, 1, 4, 7, 10
    send_x(lab_send, lab_recv, LAB)

    def gather(c, begin, end):
        def step(s, _):
            index = cells[s]
            lane = index & (size_z - 1)
            line = index // size_z
            found = jnp.zeros((kern, mark), f32)
            for h in range(row_count):
                entry = jnp.broadcast_to(table[c, h : h + 1, :], (kern, size_z))
                found = jnp.where(line == h, jnp.take_along_axis(entry, lane, axis=1), found)
            rows[c, pl.ds(s, 1), :] = jnp.sum(found * weights[s], axis=0, keepdims=True)
            return 0

        lax.fori_loop(begin, end, step, 0)

    def send_rows(c):
        z_send[c] = pick_rows(place[...], rows[c]).reshape(px, per_plane, mark)
        z_recv[c, gx] = z_send[c, gx]
        send_x(z_send.at[c], z_recv.at[c], ZS + c)

    def read_labels():
        wait_for(lab_recv, px - 1, recv_sem.at[LAB])
        parts, columns = [], []
        for n in range(total_rows // mark):
            label = jnp.sum(lab_recv[n * half : (n + 1) * half], axis=0)[0:1]
            group = lax.rem(iota((1, mark), 1), per_plane) // cap
            key = jnp.where(label > 0.5, group.astype(f32) * own + label - 1.0, -1.0)
            parts.append(key)
            columns.append(to_column(key))
        key_row = jnp.concatenate(parts, axis=1).astype(i32)
        key_col = jnp.concatenate(columns, axis=0).astype(i32)
        combine[...] = hot(iota((py * own, total_rows), 0) == key_row)
        combine_t[...] = hot(iota((total_rows, py * own), 1) == key_col)

    def send_sums(c):
        wait_for(z_recv.at[c], px - 1, recv_sem.at[ZS + c])
        d_send[c] = pick_rows(combine[...], z_recv[c].reshape(total_rows, mark)).reshape(
            py, own, mark
        )
        d_recv[c, gy] = d_send[c, gy]
        send_y(d_send.at[c], False, d_recv.at[c], DS + c)

    train_col = to_column(train[...].astype(f32))

    def send_force(c):
        wait_for(d_recv.at[c], py - 1, recv_sem.at[DS + c])
        marker_velocity = d_recv[c, 0]
        for n in range(1, py):
            marker_velocity = marker_velocity + d_recv[c, n]
        goal = jnp.zeros((own, 1), f32)
        for t in range(speed.shape[0]):
            goal = jnp.where(train_col == float(t), speed[t, c], goal)
        force = stiffness * area[...] * (goal - marker_velocity)
        force_out[:, c, :] = force
        f_all[c, gy] = force
        send_y(f_all.at[c], True, f_all.at[c], FS + c)

    def send_back(c):
        wait_for(f_all.at[c], py - 1, recv_sem.at[FS + c])
        r_send[c] = pick_rows(combine_t[...], f_all[c].reshape(py * own, mark)).reshape(
            px, per_plane, mark
        )
        r_recv[c, gx] = r_send[c, gx]
        send_x(r_send.at[c], r_recv.at[c], RS + c)

    def lane_one_hots(begin, end):
        def step(s, _):
            lane = (cells[s] & (size_z - 1)).astype(f32)
            for k in range(kern):
                wanted = jnp.broadcast_to(lane[k : k + 1, :], (16, mark)).astype(bf16)
                for j in range(size_z // 16):
                    place_of = (iota((16, mark), 0) + 16 * j).astype(f32).astype(bf16)
                    lane_hot[s, 16 * j : 16 * j + 16, k * mark : (k + 1) * mark] = jnp.where(
                        wanted == place_of, bf16(1), bf16(0)
                    )
            return 0

        lax.fori_loop(begin, end, step, 0)

    def spread(c):
        wait_for(r_recv.at[c], px - 1, recv_sem.at[RS + c])
        rows[c] = pick_rows(place_t[...], r_recv[c].reshape(total_rows, mark))

        def step(s, total):
            line = (cells[s] // size_z).astype(f32)
            value = weights[s] * rows[c, pl.ds(s, 1), :]
            high = value.astype(bf16).astype(f32)
            low = value - high
            zero = bf16(0)
            columns = []
            for k in range(kern):
                wanted = jnp.broadcast_to(line[k : k + 1, :], (16, mark)).astype(bf16)
                pieces = []
                for piece in (high, low):
                    spread_piece = jnp.broadcast_to(piece[k : k + 1, :], (16, mark)).astype(bf16)
                    for j in range(row_count // 16):
                        place_of = (iota((16, mark), 0) + 16 * j).astype(f32).astype(bf16)
                        pieces.append(jnp.where(wanted == place_of, spread_piece, zero))
                columns.append(jnp.concatenate(pieces, axis=0))
            return total + lax.dot_general(
                jnp.concatenate(columns, axis=1),
                lane_hot[s],
                (((1,), (1,)), ((), ())),
                preferred_element_type=f32,
            )

        total = lax.fori_loop(0, slots, step, jnp.zeros((2 * row_count, size_z), f32))
        cell_force[c] = (total[:row_count] + total[row_count:]).reshape(size_x, size_y, size_z)

    gather(0, 0, slots)
    send_rows(0)
    gather(1, 0, slots)
    send_rows(1)
    read_labels()
    gather(2, 0, slots // 2)
    send_sums(0)
    gather(2, slots // 2, slots)
    send_rows(2)
    send_force(0)
    lane_one_hots(0, slots // 4)
    send_back(0)
    send_sums(1)
    lane_one_hots(slots // 4, slots // 2)
    send_force(1)
    lane_one_hots(slots // 2, 3 * slots // 4)
    send_back(1)
    send_sums(2)
    lane_one_hots(3 * slots // 4, slots)
    send_force(2)
    send_back(2)
    spread(0)
    spread(1)
    spread(2)

    def relax(x, _):
        result = collide(
            [pop[q, x] for q in range(19)], [cell_force[c, x] for c in range(3)], solid[x] == 1
        )
        for q in range(19):
            relaxed[q, x] = result[q]
        return 0

    lax.fori_loop(0, size_x, relax, 0)

    lane_at = iota((size_y, size_z), 1)
    line_at = iota((size_y, size_z), 0)
    halo = []

    def send_halo(source, target, place_of):
        n = len(halo)
        copy = pltpu.make_async_remote_copy(
            src_ref=source,
            dst_ref=target,
            send_sem=halo_send.at[n],
            recv_sem=halo_recv.at[n],
            device_id=at(*place_of),
            device_id_type=MESH,
        )
        copy.start()
        halo.append(copy)

    for d, sign in enumerate((1, -1)):
        tile = jnp.zeros((size_y, size_z), f32)
        edge = size_z - 1 if sign == 1 else 0
        for n, q in enumerate(facing[2][sign]):
            for x in range(size_x):
                column = jnp.broadcast_to(relaxed[q, x][:, edge : edge + 1], (size_y, size_z))
                tile = jnp.where(lane_at == n * size_x + x, column, tile)
        t_send[d] = tile
        for side, (dx, dy) in enumerate(Z_SIDES):
            send_halo(t_send.at[d], t_recv.at[d, side], (dx, dy, sign))
    for d, sign in enumerate((1, -1)):
        edge = size_y - 1 if sign == 1 else 0
        for n, q in enumerate(facing[1][sign]):
            y_send[d, n * size_x : (n + 1) * size_x, :] = relaxed[q, :, edge, :]
        for side, dx in enumerate(Y_SIDES):
            send_halo(y_send.at[d], y_recv.at[d, side], (dx, sign, 0))
    for d, sign in enumerate((1, -1)):
        edge = size_x - 1 if sign == 1 else 0
        for n, q in enumerate(facing[0][sign]):
            x_send[d, n] = relaxed[q, edge]
        send_halo(x_send.at[d], x_recv.at[d], (sign, 0, 0))
    for copy in halo:
        copy.wait_recv()

    on_side = (
        ((line_at == 0) & (gy == 0))
        | ((line_at == size_y - 1) & (gy == py - 1))
        | ((lane_at == 0) & (gz == 0))
        | ((lane_at == size_z - 1) & (gz == pz - 1))
    )
    far = far_field()
    for q in range(19):
        cx, cy, cz = (int(v) for v in velocity_table[q])
        for x in range(size_x):
            source = x - cx
            inside = 0 <= source < size_x
            at_edge = source % size_x
            if inside:
                plane = relaxed[q, source]
            else:
                plane = x_recv[0 if cx == 1 else 1, facing[0][cx].index(q)]
            side = 0 if inside else (1 if cx == 1 else 2)
            if cy != 0:
                d = 0 if cy == 1 else 1
                n = facing[1][cy].index(q) * size_x + at_edge
                row = jnp.broadcast_to(y_recv[d, side, n : n + 1, :], (size_y, size_z))
                plane = pltpu.roll(plane, cy % size_y, 0)
                plane = jnp.where(line_at == (0 if cy == 1 else size_y - 1), row, plane)
            if cz != 0:
                d = 0 if cz == 1 else 1
                n = facing[2][cz].index(q) * size_x + at_edge
                tile = t_recv[d, side]
                if cy != 0:
                    beside = pltpu.roll(t_recv[d, 3 if cy == 1 else 4], cy % size_y, 0)
                    tile = pltpu.roll(tile, cy % size_y, 0)
                    tile = jnp.where(line_at == (0 if cy == 1 else size_y - 1), beside, tile)
                column = jnp.broadcast_to(tile[:, n : n + 1], (size_y, size_z))
                plane = pltpu.roll(plane, cz % size_z, 1)
                plane = jnp.where(lane_at == (0 if cz == 1 else size_z - 1), column, plane)
            out[q, x] = jnp.where(on_side, f32(far[q]), plane)

    wait_for(lab_send, px - 1, send_sem.at[LAB])
    for c in range(3):
        wait_for(z_send.at[c], px - 1, send_sem.at[ZS + c])
        wait_for(d_send.at[c], py - 1, send_sem.at[DS + c])
        wait_for(f_all.at[c], py - 1, send_sem.at[FS + c])
        wait_for(r_send.at[c], px - 1, send_sem.at[RS + c])
    for copy in halo:
        copy.wait_send()


def per_device(
    populations,
    solid_cells,
    slot_cells,
    slot_weights,
    slot_owner,
    slot_block,
    train_of_block,
    marker_area,
    train_velocity,
):
    px, py, pz = (lax.axis_size(axis) for axis in ("gx", "gy", "gz"))
    slots, kern, mark = slot_cells.shape[3:]
    own = train_of_block.shape[3]
    _, size_x, size_y, size_z = populations.shape
    rows_out = px * py * 2
    vmem = pl.BlockSpec(memory_space=pltpu.VMEM)
    smem = pl.BlockSpec(memory_space=pltpu.SMEM)
    face = 5 * size_x
    face_rows = -(-face // 8) * 8
    scratch = [
        pltpu.VMEM((3, size_x * size_y, size_z), f32),
        pltpu.VMEM((3, slots, mark), f32),
        pltpu.VMEM((rows_out, slots), bf16),
        pltpu.VMEM((slots, rows_out), bf16),
        pltpu.VMEM((py * own, rows_out), bf16),
        pltpu.VMEM((rows_out, py * own), bf16),
        pltpu.VMEM((px, 8, mark), f32),
        pltpu.VMEM((px, 8, mark), f32),
        pltpu.VMEM((3, px, py * 2, mark), f32),
        pltpu.VMEM((3, px, py * 2, mark), f32),
        pltpu.VMEM((3, py, own, mark), f32),
        pltpu.VMEM((3, py, own, mark), f32),
        pltpu.VMEM((3, py, own, mark), f32),
        pltpu.VMEM((3, px, py * 2, mark), f32),
        pltpu.VMEM((3, px, py * 2, mark), f32),
        pltpu.VMEM((slots, size_z, kern * mark), bf16),
        pltpu.VMEM((3, size_x, size_y, size_z), f32),
        pltpu.VMEM((19, size_x, size_y, size_z), f32),
        pltpu.VMEM((2, 5, size_y, size_z), f32),
        pltpu.VMEM((2, 5, size_y, size_z), f32),
        pltpu.VMEM((2, face_rows, size_z), f32),
        pltpu.VMEM((2, 3, face_rows, size_z), f32),
        pltpu.VMEM((2, size_y, size_z), f32),
        pltpu.VMEM((2, 5, size_y, size_z), f32),
        pltpu.SemaphoreType.DMA((13,)),
        pltpu.SemaphoreType.DMA((13,)),
        pltpu.SemaphoreType.DMA((18,)),
        pltpu.SemaphoreType.DMA((18,)),
    ]
    populations_next, marker_force = pl.pallas_call(
        functools.partial(kernel, px, py, pz),
        out_shape=(
            jax.ShapeDtypeStruct(populations.shape, f32),
            jax.ShapeDtypeStruct((own, 3, mark), f32),
        ),
        in_specs=[vmem] * 8 + [smem],
        out_specs=(vmem, vmem),
        scratch_shapes=scratch,
        compiler_params=pltpu.CompilerParams(
            collective_id=0, has_side_effects=True, vmem_limit_bytes=48 << 20
        ),
        name="step",
    )(
        populations,
        solid_cells,
        slot_cells.reshape(slots, kern, mark),
        slot_weights.reshape(slots, kern, mark),
        slot_owner.reshape(1, slots),
        slot_block.reshape(1, slots),
        train_of_block.reshape(1, own),
        marker_area.reshape(own, mark),
        train_velocity,
    )
    return (populations_next, marker_force.reshape(1, 1, 1, own, 3, mark))


def solution(mesh):
    placed = (
        P(None, "gx", "gy", "gz"),
        P("gx", "gy", "gz"),
        P("gx", "gy", "gz", None, None, None),
        P("gx", "gy", "gz", None, None, None),
        P("gx", "gy", "gz", None, None),
        P("gx", "gy", "gz", None),
        P("gx", "gy", "gz", None),
        P("gx", "gy", "gz", None, None),
        P(),
    )
    return jax.shard_map(
        per_device,
        mesh=mesh,
        in_specs=placed,
        out_specs=(P(None, "gx", "gy", "gz"), P("gx", "gy", "gz", None, None, None)),
        check_vma=False,
    )
```

time: 718 us -> 120 us (0.17)
  other arithmetic: 364 us -> 0 us
  local copies, waits for them, and re-layouts: 233 us -> 6.31 us
  Pallas kernels: 0 us -> 112 us
  starting transfers between devices: 61.2 us -> 0 us
  waiting for transfers between devices: 56.3 us -> 0 us
    scatter-add x1 -> x0, other arithmetic: 316 us -> none  [per_device(): jnp.zeros((3, cell_count), jnp.float32).at[:, cells.reshape(-1)]]
    gather x1 -> x0, local copies, waits for them, and re-layouts: 216 us -> none  [per_device(): partial_value = jnp.sum(rest_velocity[:, cells] * weights[None], axis=2)]
    pallas_call x0 -> x1, Pallas kernels: none -> 112 us  [per_device(): pl.pallas_call(functools.partial(kernel, px, py, pz), out_shape=(jax.Shap...]
    all_to_all x3 -> x0, waiting for transfers between devices: 48.8 us -> none  [the longest x1 25.1 us: per_device(): lax.all_to_all(back_rows.reshape(peers, capacity, 3 * mark), ('gx', 'gy')...]
    all_to_all x3 -> x0, starting transfers between devices: 45.4 us -> none  [the longest x1 20.4 us: per_device(): lax.all_to_all(labels.reshape(peers, capacity), ('gx', 'gy'), split_axis=...]
    ppermute x6 -> x0, starting transfers between devices: 15.8 us -> none  [the longest x3 10.5 us: with_halo(): lax.ppermute(tail, axis, [(i, (i + 1) % count) for i in range(count)])]
    reduce_sum x3 -> x0, other arithmetic: 15 us -> none  [the longest x1 14 us: per_device(): partial_value = jnp.sum(rest_velocity[:, cells] * weights[None], axis=2)]
    mul x2 -> x0, other arithmetic: 12.8 us -> none  [the longest x1 12.8 us: per_device(): contrib = weights[None] * slot_force[:, :, None, :]]
  transfers between devices with their start and end apart: 9 -> 0, of which waited for: 5 -> 0; matrix products, arithmetic and copies ran while one was open for 34% -> 0% of each run, Pallas kernels for 0% -> 0%
where the time goes in v1:
time: 120 us; the launch traced here: 119 us
  Pallas kernels  112 us (93%)
  local copies, waits for them, and re-layouts  6.31 us (5%)
    pallas_call x1, Pallas kernels, per_device(): pl.pallas_call(functools.partial(kernel, px, py, pz), out_shape=(jax.Shap...  112 us
    unnamed x20, local copies, waits for them, and re-layouts  6.31 us

profile of v1, /device:TPU:1, one launch (start us, length us, event | category | flops | bytes accessed | tf_op | source)
XLA Modules:
  0.0 119.4 jit_solution(4015909431858498563)
XLA Ops:
  0.6 0.0 copy-start.5
  0.6 0.0 copy-start.6
  0.7 0.0 copy-start.7
  0.7 0.0 copy-start.8
  0.7 0.6 copy-done.5
  1.3 0.0 copy-done.6
  1.3 0.0 copy-done.7
  1.3 0.0 copy-done.8
  1.3 0.0 copy-start
  1.3 1.0 copy-done
  2.3 0.0 copy-start.1
  2.3 0.9 copy-done.1
  3.3 0.0 copy-start.2
  3.3 0.9 copy-done.2
  4.2 0.0 copy-start.3
  4.2 0.7 copy-done.3
  4.9 0.0 copy-start.4
  4.9 0.7 copy-done.4
  5.6 112.4 %step.1 = (f32[19,4,8,128]{3,2,1,0:T(8,128)S(1)}, f32[32,3,128]{2,1,0:T(4,128)S(1)}) custom-call(f32[19,4,8,128]{3,2,1,0:T(8,128)S(1)} %copy-done, s32[4,8,128]{2,1,0:T(8,128)S(1)} %copy-done.3, s32[64,8,128]{2,1,0:T(8,128)S(1)} %bitcast.7, f32[64,8,128]{2,1,0:T(8,128)S(1)} %bitcast.8, s32[1,64]{1,0:T(1,128)S(1)} %bitcast.11, s32[1,64]{1,0:T(1,128)S(1)} %bitcast.12, ...), custom_call_target="tpu_custom_call" | custom-call | tf_op jit(solution)/shard_map/step/pallas_call | solution.py:596
  118.0 0.6 copy.11
  118.7 0.7 copy.13
Async XLA Ops:
  0.6 0.7 copy-start.5
  0.6 0.7 copy-start.6
  0.7 0.7 copy-start.7
  0.7 0.7 copy-start.8
  1.3 1.0 copy-start
  2.3 0.9 copy-start.1
  3.3 0.9 copy-start.2
  4.2 0.7 copy-start.3
  4.9 0.7 copy-start.4

commit v2 on v1

--- a/solution.py
+++ b/solution.py
@@ -172,6 +172,17 @@
     px,
     py,
     pz,
+    pop_in,
+    solid_in,
+    cells_in,
+    weights_in,
+    owner_in,
+    block_in,
+    train_in,
+    area_in,
+    speed_in,
+    out,
+    force_out,
     pop,
     solid,
     cells,
@@ -181,8 +192,6 @@
     train,
     area,
     speed,
-    out,
-    force_out,
     table,
     rows,
     place,
@@ -198,7 +207,7 @@
     f_all,
     r_send,
     r_recv,
-    lane_hot,
+    point_hot,
     cell_force,
     relaxed,
     x_send,
@@ -211,6 +220,7 @@
     recv_sem,
     halo_send,
     halo_recv,
+    load_sem,
 ):
     slots, kern, mark = cells.shape
     size_x, size_y, size_z = pop.shape[1:]
@@ -234,6 +244,24 @@
         + [(a, 0, b) for a in (1, -1) for b in (1, -1)]
         + [(0, a, b) for a in (1, -1) for b in (1, -1)]
     )
+    loads = [
+        pltpu.make_async_copy(source, target, load_sem.at[n])
+        for n, (source, target) in enumerate(
+            (
+                (owner_in, owner),
+                (block_in, block),
+                (pop_in, pop),
+                (cells_in, cells),
+                (weights_in, weights),
+                (train_in, train),
+                (area_in, area),
+                (speed_in, speed),
+                (solid_in, solid),
+            )
+        )
+    ]
+    for load in loads:
+        load.start()
     barrier = pltpu.get_barrier_semaphore()
 
     def greet_x(k, _):
@@ -249,6 +277,8 @@
     for place_of in halo_far:
         pl.semaphore_signal(barrier, inc=1, device_id=at(*place_of), device_id_type=MESH)
 
+    loads[0].wait()
+    loads[1].wait()
     owner_row = owner[...].astype(f32)
     owner_col = to_column(owner_row)
     same = owner_col == owner_row
@@ -268,11 +298,11 @@
     lab_send[...] = jnp.broadcast_to(labels[:, None, :], lab_send.shape)
     lab_recv[gx] = lab_send[gx]
 
+    loads[2].wait()
     density, momentum = moments([pop[q] for q in range(19)])
     for c in range(3):
         table[c] = (momentum[c] / density).reshape(row_count, size_z)
 
-    pl.semaphore_wait(barrier, px - 1 + py - 1 + len(halo_far))
 
     def send_x(source, target, stage):
         def step(i, _):
@@ -310,9 +340,10 @@
         pltpu.make_async_copy(part, part, semaphore).wait()
 
     LAB, ZS, DS, FS, RS = 0, 1, 4, 7, 10
+    pl.semaphore_wait(barrier, px - 1 + py - 1 + len(halo_far))
     send_x(lab_send, lab_recv, LAB)
 
-    def gather(c, begin, end):
+    def gather(c):
         def step(s, _):
             index = cells[s]
             lane = index & (size_z - 1)
@@ -324,7 +355,7 @@
             rows[c, pl.ds(s, 1), :] = jnp.sum(found * weights[s], axis=0, keepdims=True)
             return 0
 
-        lax.fori_loop(begin, end, step, 0)
+        lax.fori_loop(0, slots, step, 0, unroll=8)
 
     def send_rows(c):
         z_send[c] = pick_rows(place[...], rows[c]).reshape(px, per_plane, mark)
@@ -353,6 +384,8 @@
         d_recv[c, gy] = d_send[c, gy]
         send_y(d_send.at[c], False, d_recv.at[c], DS + c)
 
+    for load in loads[5:]:
+        load.wait()
     train_col = to_column(train[...].astype(f32))
 
     def send_force(c):
@@ -364,7 +397,7 @@
         for t in range(speed.shape[0]):
             goal = jnp.where(train_col == float(t), speed[t, c], goal)
         force = stiffness * area[...] * (goal - marker_velocity)
-        force_out[:, c, :] = force
+        force_out[c] = force
         f_all[c, gy] = force
         send_y(f_all.at[c], True, f_all.at[c], FS + c)
 
@@ -376,19 +409,19 @@
         r_recv[c, gx] = r_send[c, gx]
         send_x(r_send.at[c], r_recv.at[c], RS + c)
 
-    def lane_one_hots(begin, end):
+    def point_one_hots(begin, end):
         def step(s, _):
             lane = (cells[s] & (size_z - 1)).astype(f32)
+            columns = jnp.transpose(jnp.concatenate([lane] * (mark // kern), axis=0))
+            place_of = iota((mark, size_z), 1).astype(f32).astype(bf16)
             for k in range(kern):
-                wanted = jnp.broadcast_to(lane[k : k + 1, :], (16, mark)).astype(bf16)
-                for j in range(size_z // 16):
-                    place_of = (iota((16, mark), 0) + 16 * j).astype(f32).astype(bf16)
-                    lane_hot[s, 16 * j : 16 * j + 16, k * mark : (k + 1) * mark] = jnp.where(
-                        wanted == place_of, bf16(1), bf16(0)
-                    )
+                wanted = jnp.broadcast_to(columns[:, k : k + 1], (mark, size_z)).astype(bf16)
+                point_hot[s, k * mark : (k + 1) * mark, :] = jnp.where(
+                    wanted == place_of, bf16(1), bf16(0)
+                )
             return 0
 
-        lax.fori_loop(begin, end, step, 0)
+        lax.fori_loop(begin, end, step, 0, unroll=4)
 
     def spread(c):
         wait_for(r_recv.at[c], px - 1, recv_sem.at[RS + c])
@@ -410,35 +443,35 @@
                         place_of = (iota((16, mark), 0) + 16 * j).astype(f32).astype(bf16)
                         pieces.append(jnp.where(wanted == place_of, spread_piece, zero))
                 columns.append(jnp.concatenate(pieces, axis=0))
-            return total + lax.dot_general(
-                jnp.concatenate(columns, axis=1),
-                lane_hot[s],
-                (((1,), (1,)), ((), ())),
-                preferred_element_type=f32,
+            return total + jnp.dot(
+                jnp.concatenate(columns, axis=1), point_hot[s], preferred_element_type=f32
             )
 
-        total = lax.fori_loop(0, slots, step, jnp.zeros((2 * row_count, size_z), f32))
+        total = lax.fori_loop(
+            0, slots, step, jnp.zeros((2 * row_count, size_z), f32), unroll=8
+        )
         cell_force[c] = (total[:row_count] + total[row_count:]).reshape(size_x, size_y, size_z)
 
-    gather(0, 0, slots)
+    loads[3].wait()
+    loads[4].wait()
+    gather(0)
     send_rows(0)
-    gather(1, 0, slots)
+    gather(1)
     send_rows(1)
     read_labels()
-    gather(2, 0, slots // 2)
+    gather(2)
+    send_rows(2)
     send_sums(0)
-    gather(2, slots // 2, slots)
-    send_rows(2)
+    point_one_hots(0, slots // 4)
     send_force(0)
-    lane_one_hots(0, slots // 4)
+    point_one_hots(slots // 4, slots // 2)
     send_back(0)
     send_sums(1)
-    lane_one_hots(slots // 4, slots // 2)
+    point_one_hots(slots // 2, 3 * slots // 4)
     send_force(1)
-    lane_one_hots(slots // 2, 3 * slots // 4)
+    point_one_hots(3 * slots // 4, slots)
     send_back(1)
     send_sums(2)
-    lane_one_hots(3 * slots // 4, slots)
     send_force(2)
     send_back(2)
     spread(0)
@@ -560,10 +593,19 @@
     _, size_x, size_y, size_z = populations.shape
     rows_out = px * py * 2
     vmem = pl.BlockSpec(memory_space=pltpu.VMEM)
-    smem = pl.BlockSpec(memory_space=pltpu.SMEM)
+    hbm = pl.BlockSpec(memory_space=pltpu.HBM)
     face = 5 * size_x
     face_rows = -(-face // 8) * 8
     scratch = [
+        pltpu.VMEM(populations.shape, f32),
+        pltpu.VMEM(solid_cells.shape, i32),
+        pltpu.VMEM((slots, kern, mark), i32),
+        pltpu.VMEM((slots, kern, mark), f32),
+        pltpu.VMEM((1, slots), i32),
+        pltpu.VMEM((1, slots), i32),
+        pltpu.VMEM((1, own), i32),
+        pltpu.VMEM((own, mark), f32),
+        pltpu.SMEM(train_velocity.shape, f32),
         pltpu.VMEM((3, size_x * size_y, size_z), f32),
         pltpu.VMEM((3, slots, mark), f32),
         pltpu.VMEM((rows_out, slots), bf16),
@@ -579,7 +621,7 @@
         pltpu.VMEM((3, py, own, mark), f32),
         pltpu.VMEM((3, px, py * 2, mark), f32),
         pltpu.VMEM((3, px, py * 2, mark), f32),
-        pltpu.VMEM((slots, size_z, kern * mark), bf16),
+        pltpu.VMEM((slots, kern * mark, size_z), bf16),
         pltpu.VMEM((3, size_x, size_y, size_z), f32),
         pltpu.VMEM((19, size_x, size_y, size_z), f32),
         pltpu.VMEM((2, 5, size_y, size_z), f32),
@@ -592,18 +634,19 @@
         pltpu.SemaphoreType.DMA((13,)),
         pltpu.SemaphoreType.DMA((18,)),
         pltpu.SemaphoreType.DMA((18,)),
+        pltpu.SemaphoreType.DMA((9,)),
     ]
     populations_next, marker_force = pl.pallas_call(
         functools.partial(kernel, px, py, pz),
         out_shape=(
             jax.ShapeDtypeStruct(populations.shape, f32),
-            jax.ShapeDtypeStruct((own, 3, mark), f32),
+            jax.ShapeDtypeStruct((3, own, mark), f32),
         ),
-        in_specs=[vmem] * 8 + [smem],
+        in_specs=[hbm] * 9,
         out_specs=(vmem, vmem),
         scratch_shapes=scratch,
         compiler_params=pltpu.CompilerParams(
-            collective_id=0, has_side_effects=True, vmem_limit_bytes=48 << 20
+            collective_id=0, has_side_effects=True, vmem_limit_bytes=60 << 20
         ),
         name="step",
     )(
@@ -617,7 +660,7 @@
         marker_area.reshape(own, mark),
         train_velocity,
     )
-    return (populations_next, marker_force.reshape(1, 1, 1, own, 3, mark))
+    return (populations_next, marker_force.transpose(1, 0, 2).reshape(1, 1, 1, own, 3, mark))
 
 
 def solution(mesh):

time: 120 us -> 79 us (0.66)
  Pallas kernels: 112 us -> 75.9 us
  local copies, waits for them, and re-layouts: 6.31 us -> 2.34 us
    pallas_call x1, Pallas kernels: 112 us -> 75.9 us  [per_device(): pl.pallas_call(functools.partial(kernel, px, py, pz), out_shape=(jax.Shap...]
    unnamed x20 -> x4, local copies, waits for them, and re-layouts: 6.31 us -> 2.34 us
where the time goes in v2:
time: 79 us; the launch traced here: 78.9 us
  Pallas kernels  75.9 us (96%)
  local copies, waits for them, and re-layouts  2.34 us (3%)
    pallas_call x1, Pallas kernels, per_device(): pl.pallas_call(functools.partial(kernel, px, py, pz), out_shape=(jax.Shap...  75.9 us
    unnamed x4, local copies, waits for them, and re-layouts  2.34 us

profile of v2, /device:TPU:1, one launch (start us, length us, event | category | flops | bytes accessed | tf_op | source)
XLA Modules:
  0.0 78.9 jit_solution(6978698118923111497)
XLA Ops:
  0.6 75.9 %step.1 = (f32[19,4,8,128]{3,2,1,0:T(8,128)}, f32[3,32,128]{2,1,0:T(8,128)}) custom-call(f32[19,4,8,128]{3,2,1,0:T(8,128)} %pop_in.1, s32[4,8,128]{2,1,0:T(8,128)} %solid_in.1, s32[64,8,128]{2,1,0:T(8,128)} %bitcast.9, f32[64,8,128]{2,1,0:T(8,128)} %bitcast.10, s32[1,64]{1,0:T(1,128)} %bitcast.13, s32[1,64]{1,0:T(1,128)} %bitcast.14, s32[1,32]{1,0:T(1,128)} %bitcast.15, ...), custom_call_target="tpu_custom_call" | custom-call | tf_op jit(solution)/shard_map/step/pallas_call | solution.py:639
  76.5 0.0 copy-start
  76.5 1.7 %copy.13 = f32[19,4,8,128]{3,2,1,0:T(8,128)} copy(f32[19,4,8,128]{3,2,1,0:T(8,128)} %get-tuple-element.8) | data formatting | bytes 622592
  78.3 0.0 copy-done
  78.3 0.6 copy.14
Async XLA Ops:
  76.5 1.7 %copy-start = (f32[3,32,128]{2,1,0:T(8,128)S(1)}, f32[3,32,128]{2,1,0:T(8,128)}, u32[]{:S(2)}) copy-start(f32[3,32,128]{2,1,0:T(8,128)} %get-tuple-element.5) | copy-start | bytes 147460

commit v3 on v2

--- a/solution.py
+++ b/solution.py
@@ -295,7 +295,8 @@
     spot = lax.rem(target_col, per_plane) + per_plane * lax.rem(gx, half)
     label_hot = jnp.where(iota((slots, mark), 1) == spot, label_col, 0.0).astype(bf16)
     labels = jnp.dot(plane_hot, label_hot, preferred_element_type=f32)
-    lab_send[...] = jnp.broadcast_to(labels[:, None, :], lab_send.shape)
+    for n in range(px):
+        lab_send[n] = labels[n : n + 1]
     lab_recv[gx] = lab_send[gx]
 
     loads[2].wait()
@@ -321,7 +322,8 @@
         lax.fori_loop(0, px - 1, step, 0)
 
     def send_y(source, own_place, target, stage):
-        def step(k, _):
+        def step(i, _):
+            k = py // 2 + ((i + 1) // 2) * (1 - 2 * lax.rem(i, 2))
             peer = at(0, k, 0)
             pltpu.make_async_remote_copy(
                 src_ref=source.at[gy if own_place else peer[1]],
@@ -333,15 +335,13 @@
             ).start()
             return 0
 
-        lax.fori_loop(1, py, step, 0)
+        lax.fori_loop(0, py - 1, step, 0)
 
     def wait_for(buffer, count, semaphore):
         part = buffer.at[pl.ds(0, count)]
         pltpu.make_async_copy(part, part, semaphore).wait()
 
     LAB, ZS, DS, FS, RS = 0, 1, 4, 7, 10
-    pl.semaphore_wait(barrier, px - 1 + py - 1 + len(halo_far))
-    send_x(lab_send, lab_recv, LAB)
 
     def gather(c):
         def step(s, _):
@@ -366,7 +366,7 @@
         wait_for(lab_recv, px - 1, recv_sem.at[LAB])
         parts, columns = [], []
         for n in range(total_rows // mark):
-            label = jnp.sum(lab_recv[n * half : (n + 1) * half], axis=0)[0:1]
+            label = jnp.sum(lab_recv[n * half : (n + 1) * half], axis=0)
             group = lax.rem(iota((1, mark), 1), per_plane) // cap
             key = jnp.where(label > 0.5, group.astype(f32) * own + label - 1.0, -1.0)
             parts.append(key)
@@ -448,13 +448,15 @@
             )
 
         total = lax.fori_loop(
-            0, slots, step, jnp.zeros((2 * row_count, size_z), f32), unroll=8
+            0, slots, step, jnp.zeros((2 * row_count, size_z), f32), unroll=16
         )
         cell_force[c] = (total[:row_count] + total[row_count:]).reshape(size_x, size_y, size_z)
 
     loads[3].wait()
     loads[4].wait()
     gather(0)
+    pl.semaphore_wait(barrier, px - 1 + py - 1 + len(halo_far))
+    send_x(lab_send, lab_recv, LAB)
     send_rows(0)
     gather(1)
     send_rows(1)
@@ -462,31 +464,28 @@
     gather(2)
     send_rows(2)
     send_sums(0)
-    point_one_hots(0, slots // 4)
+    point_one_hots(0, 16)
     send_force(0)
-    point_one_hots(slots // 4, slots // 2)
+    point_one_hots(16, 32)
+    send_sums(1)
+    point_one_hots(32, 48)
+    send_force(1)
+    send_sums(2)
     send_back(0)
-    send_sums(1)
-    point_one_hots(slots // 2, 3 * slots // 4)
-    send_force(1)
-    point_one_hots(3 * slots // 4, slots)
     send_back(1)
-    send_sums(2)
+    point_one_hots(48, 64)
     send_force(2)
     send_back(2)
     spread(0)
     spread(1)
     spread(2)
 
-    def relax(x, _):
+    def relax(x):
         result = collide(
             [pop[q, x] for q in range(19)], [cell_force[c, x] for c in range(3)], solid[x] == 1
         )
         for q in range(19):
             relaxed[q, x] = result[q]
-        return 0
-
-    lax.fori_loop(0, size_x, relax, 0)
 
     lane_at = iota((size_y, size_z), 1)
     line_at = iota((size_y, size_z), 0)
@@ -505,6 +504,15 @@
         copy.start()
         halo.append(copy)
 
+    relax(0)
+    relax(size_x - 1)
+    for d, sign in enumerate((1, -1)):
+        edge = size_x - 1 if sign == 1 else 0
+        for n, q in enumerate(facing[0][sign]):
+            x_send[d, n] = relaxed[q, edge]
+        send_halo(x_send.at[d], x_recv.at[d], (sign, 0, 0))
+    for x in range(1, size_x - 1):
+        relax(x)
     for d, sign in enumerate((1, -1)):
         tile = jnp.zeros((size_y, size_z), f32)
         edge = size_z - 1 if sign == 1 else 0
@@ -513,19 +521,14 @@
                 column = jnp.broadcast_to(relaxed[q, x][:, edge : edge + 1], (size_y, size_z))
                 tile = jnp.where(lane_at == n * size_x + x, column, tile)
         t_send[d] = tile
-        for side, (dx, dy) in enumerate(Z_SIDES):
+        for side, (dx, dy) in reversed(list(enumerate(Z_SIDES))):
             send_halo(t_send.at[d], t_recv.at[d, side], (dx, dy, sign))
     for d, sign in enumerate((1, -1)):
         edge = size_y - 1 if sign == 1 else 0
         for n, q in enumerate(facing[1][sign]):
             y_send[d, n * size_x : (n + 1) * size_x, :] = relaxed[q, :, edge, :]
-        for side, dx in enumerate(Y_SIDES):
+        for side, dx in reversed(list(enumerate(Y_SIDES))):
             send_halo(y_send.at[d], y_recv.at[d, side], (dx, sign, 0))
-    for d, sign in enumerate((1, -1)):
-        edge = size_x - 1 if sign == 1 else 0
-        for n, q in enumerate(facing[0][sign]):
-            x_send[d, n] = relaxed[q, edge]
-        send_halo(x_send.at[d], x_recv.at[d], (sign, 0, 0))
     for copy in halo:
         copy.wait_recv()
 
@@ -612,8 +615,8 @@
         pltpu.VMEM((slots, rows_out), bf16),
         pltpu.VMEM((py * own, rows_out), bf16),
         pltpu.VMEM((rows_out, py * own), bf16),
-        pltpu.VMEM((px, 8, mark), f32),
-        pltpu.VMEM((px, 8, mark), f32),
+        pltpu.VMEM((px, 1, mark), f32),
+        pltpu.VMEM((px, 1, mark), f32),
         pltpu.VMEM((3, px, py * 2, mark), f32),
         pltpu.VMEM((3, px, py * 2, mark), f32),
         pltpu.VMEM((3, py, own, mark), f32),
@@ -639,8 +642,8 @@
     populations_next, marker_force = pl.pallas_call(
         functools.partial(kernel, px, py, pz),
         out_shape=(
-            jax.ShapeDtypeStruct(populations.shape, f32),
-            jax.ShapeDtypeStruct((3, own, mark), f32),
+            pltpu.VMEM(populations.shape, f32),
+            pltpu.VMEM((3, own, mark), f32),
         ),
         in_specs=[hbm] * 9,
         out_specs=(vmem, vmem),

time: 79 us -> 70.4 us (0.89)
  Pallas kernels: 75.9 us -> 68.3 us
  local copies, waits for them, and re-layouts: 2.34 us -> 1.34 us
    pallas_call x1, Pallas kernels: 75.9 us -> 68.3 us  [per_device(): pl.pallas_call(functools.partial(kernel, px, py, pz), out_shape=(pltpu.VM...]
    unnamed x4 -> x2, local copies, waits for them, and re-layouts: 2.34 us -> 1.34 us
where the time goes in v3:
time: 70.4 us; the launch traced here: 70.2 us
  Pallas kernels  68.3 us (97%)
  local copies, waits for them, and re-layouts  1.34 us (2%)
    pallas_call x1, Pallas kernels, per_device(): pl.pallas_call(functools.partial(kernel, px, py, pz), out_shape=(pltpu.VM...  68.3 us

profile of v3, /device:TPU:1, one launch (start us, length us, event | category | flops | bytes accessed | tf_op | source)
XLA Modules:
  0.0 70.2 jit_solution(12586617840472850644)
XLA Ops:
  0.6 68.3 %step.1 = (f32[19,4,8,128]{3,2,1,0:T(8,128)S(1)}, f32[3,32,128]{2,1,0:T(8,128)S(1)}) custom-call(f32[19,4,8,128]{3,2,1,0:T(8,128)} %pop_in.1, s32[4,8,128]{2,1,0:T(8,128)} %solid_in.1, s32[64,8,128]{2,1,0:T(8,128)} %bitcast.10, f32[64,8,128]{2,1,0:T(8,128)} %bitcast.11, s32[1,64]{1,0:T(1,128)} %bitcast.13, s32[1,64]{1,0:T(1,128)} %bitcast.14, ...), custom_call_target="tpu_custom_call" | custom-call | tf_op jit(solution)/shard_map/step/pallas_call | solution.py:642
  68.9 0.7 %copy.13 = f32[19,4,8,128]{3,2,1,0:T(8,128)} copy(f32[19,4,8,128]{3,2,1,0:T(8,128)S(1)} %get-tuple-element.6) | data formatting | bytes 622592
  69.6 0.6 copy.14

commit v4 on v3

--- a/solution.py
+++ b/solution.py
@@ -149,9 +149,10 @@
     rest = values - high.astype(f32)
     middle = rest.astype(bf16)
     low = (rest - middle.astype(f32)).astype(bf16)
-    total = jnp.dot(one_hot, low, preferred_element_type=f32)
-    total = total + jnp.dot(one_hot, middle, preferred_element_type=f32)
-    return total + jnp.dot(one_hot, high, preferred_element_type=f32)
+    pieces = jnp.concatenate([low, middle, high], axis=1)
+    found = jnp.dot(one_hot, pieces, preferred_element_type=f32)
+    n = values.shape[1]
+    return found[:, :n] + found[:, n : 2 * n] + found[:, 2 * n :]
 
 
 def iota(shape, dim):
@@ -401,12 +402,14 @@
         f_all[c, gy] = force
         send_y(f_all.at[c], True, f_all.at[c], FS + c)
 
-    def send_back(c):
+    def make_back(c):
         wait_for(f_all.at[c], py - 1, recv_sem.at[FS + c])
         r_send[c] = pick_rows(combine_t[...], f_all[c].reshape(py * own, mark)).reshape(
             px, per_plane, mark
         )
         r_recv[c, gx] = r_send[c, gx]
+
+    def send_back(c):
         send_x(r_send.at[c], r_recv.at[c], RS + c)
 
     def point_one_hots(begin, end):
@@ -464,17 +467,20 @@
     gather(2)
     send_rows(2)
     send_sums(0)
-    point_one_hots(0, 16)
+    point_one_hots(0 * slots // 4, 1 * slots // 4)
     send_force(0)
-    point_one_hots(16, 32)
     send_sums(1)
-    point_one_hots(32, 48)
-    send_force(1)
+    point_one_hots(1 * slots // 4, 2 * slots // 4)
+    point_one_hots(2 * slots // 4, 3 * slots // 4)
+    make_back(0)
     send_sums(2)
     send_back(0)
+    send_force(1)
+    point_one_hots(3 * slots // 4, 4 * slots // 4)
+    make_back(1)
     send_back(1)
-    point_one_hots(48, 64)
     send_force(2)
+    make_back(2)
     send_back(2)
     spread(0)
     spread(1)

time: 70.4 us -> 68.3 us (0.970)
  Pallas kernels: 68.3 us -> 66.2 us
    pallas_call x1, Pallas kernels: 68.3 us -> 66.2 us  [per_device(): pl.pallas_call(functools.partial(kernel, px, py, pz), out_shape=(pltpu.VM...]
where the time goes in v4:
time: 68.3 us; the launch traced here: 68.1 us
  Pallas kernels  66.2 us (97%)
  local copies, waits for them, and re-layouts  1.34 us (2%)
    pallas_call x1, Pallas kernels, per_device(): pl.pallas_call(functools.partial(kernel, px, py, pz), out_shape=(pltpu.VM...  66.2 us

profile of v4, /device:TPU:1, one launch (start us, length us, event | category | flops | bytes accessed | tf_op | source)
XLA Modules:
  0.0 68.1 jit_solution(12312525089844749538)
XLA Ops:
  0.6 66.2 %step.1 = (f32[19,4,8,128]{3,2,1,0:T(8,128)S(1)}, f32[3,32,128]{2,1,0:T(8,128)S(1)}) custom-call(f32[19,4,8,128]{3,2,1,0:T(8,128)} %pop_in.1, s32[4,8,128]{2,1,0:T(8,128)} %solid_in.1, s32[64,8,128]{2,1,0:T(8,128)} %bitcast.10, f32[64,8,128]{2,1,0:T(8,128)} %bitcast.11, s32[1,64]{1,0:T(1,128)} %bitcast.13, s32[1,64]{1,0:T(1,128)} %bitcast.14, ...), custom_call_target="tpu_custom_call" | custom-call | tf_op jit(solution)/shard_map/step/pallas_call | solution.py:648
  66.8 0.7 %copy.13 = f32[19,4,8,128]{3,2,1,0:T(8,128)} copy(f32[19,4,8,128]{3,2,1,0:T(8,128)S(1)} %get-tuple-element.6) | data formatting | bytes 622592
  67.5 0.6 copy.14

commit v5 on v4

--- a/solution.py
+++ b/solution.py
@@ -463,9 +463,9 @@
     send_rows(0)
     gather(1)
     send_rows(1)
-    read_labels()
     gather(2)
     send_rows(2)
+    read_labels()
     send_sums(0)
     point_one_hots(0 * slots // 4, 1 * slots // 4)
     send_force(0)

time: 68.3 us -> 68.5 us (level)
  no operation moved by 1% of the time
where the time goes in v5:
time: 68.5 us; the launch traced here: 68.4 us
  Pallas kernels  66.4 us (97%)
  local copies, waits for them, and re-layouts  1.34 us (2%)
    pallas_call x1, Pallas kernels, per_device(): pl.pallas_call(functools.partial(kernel, px, py, pz), out_shape=(pltpu.VM...  66.4 us

profile of v5, /device:TPU:1, one launch (start us, length us, event | category | flops | bytes accessed | tf_op | source)
XLA Modules:
  0.0 68.4 jit_solution(15602803518390349849)
XLA Ops:
  0.6 66.4 %step.1 = (f32[19,4,8,128]{3,2,1,0:T(8,128)S(1)}, f32[3,32,128]{2,1,0:T(8,128)S(1)}) custom-call(f32[19,4,8,128]{3,2,1,0:T(8,128)} %pop_in.1, s32[4,8,128]{2,1,0:T(8,128)} %solid_in.1, s32[64,8,128]{2,1,0:T(8,128)} %bitcast.10, f32[64,8,128]{2,1,0:T(8,128)} %bitcast.11, s32[1,64]{1,0:T(1,128)} %bitcast.13, s32[1,64]{1,0:T(1,128)} %bitcast.14, ...), custom_call_target="tpu_custom_call" | custom-call | tf_op jit(solution)/shard_map/step/pallas_call | solution.py:648
  67.1 0.7 %copy.13 = f32[19,4,8,128]{3,2,1,0:T(8,128)} copy(f32[19,4,8,128]{3,2,1,0:T(8,128)S(1)} %get-tuple-element.6) | data formatting | bytes 622592
  67.8 0.6 copy.14
